TPU v7x, 128 devices: a whole 4x4x4 slice. The times are simulated.
128 devices in a mesh: silo: 8 (over z, core), row: 16 (over y, x).
Axes of the slice: x: 4, y: 4, z: 4, core: 2. Of those that a mesh axis runs over, the one named last changes fastest.
Arguments:
- silo_grams: float32 [16, 4096, 4096], P('silo', 'row'), may hold values from -9 to 81, as said below
- silo_weights: bfloat16 [16, 4096, 640], P('silo', 'row'), may hold values from -6 to 6
Outputs:
- merged_rows: float32 [640, 4096], P(('silo', 'row'))
Inputs may be any that keep to these rules, and one draw needn't show every extreme that they name: `silo_grams`: each silo's Gram is symmetric up to float32 rounding and positive definite.
All inputs are finite; a program needn't handle non-finite values.
Results may differ from a plain program's by a relative error of at most 0.0003.
Values may be sent and summed in bfloat16 or wider, within the bound.
A program may use at most 128 MiB of HBM per device.

v0:
```python
import jax
import jax.numpy as jnp
from jax import lax
from jax.sharding import Mesh
from jax.sharding import PartitionSpec as P

ITERS = 2
ROW = ("row_0", "row_1")
SILO_ROW = ("silo", "row_0", "row_1")
full_precision = lax.Precision.HIGHEST


def in_blocks(value, dim, peers):
    lengths = value.shape
    parts = value.reshape(*lengths[:dim], peers, lengths[dim] // peers, *lengths[dim + 1 :])
    return jnp.moveaxis(parts, dim, 0)


def summed_on_arrival(value, axis, dim):
    parts = in_blocks(value, dim, lax.axis_size(axis))
    arrived = lax.all_to_all(parts, axis, split_axis=0, concat_axis=0, tiled=True)
    return arrived.sum(axis=0)


def joined_along(parts, dim):
    lengths = list(parts.shape[1:])
    lengths[dim] *= parts.shape[0]
    return jnp.moveaxis(parts, 0, dim).reshape(lengths)


def sent_to_all(value, axis):
    copies = jnp.broadcast_to(value, (lax.axis_size(axis), *value.shape))
    return lax.all_to_all(copies, axis, split_axis=0, concat_axis=0, tiled=True)


def gathered_copies(value, axis, dim):
    return joined_along(sent_to_all(value, axis), dim)


def one_axis_at_a_time(value, axes):
    for axis in axes:
        value = lax.psum(value, axis)
    return value


def conj_grad(right_side, apply_op, sum_squares, sum_curv):
    solution = jnp.zeros_like(right_side)
    residual = right_side
    direction = right_side
    res_norm = sum_squares(jnp.sum(residual * residual, axis=0))
    for iteration in range(ITERS):
        mapped = apply_op(direction)
        step_size = res_norm / sum_curv(jnp.sum(direction * mapped, axis=0))
        solution = solution + step_size * direction
        residual = residual - step_size * mapped
        if iteration + 1 < ITERS:
            next_norm = sum_squares(jnp.sum(residual * residual, axis=0))
            direction = residual + next_norm / res_norm * direction
            res_norm = next_norm
    return solution


def local(silo_grams, silo_weights):
    partial_op = jnp.sum(silo_grams, axis=0)
    partial_rhs = jnp.einsum(
        "srk,skc->rc",
        silo_grams,
        lax.all_gather(silo_weights, ROW, axis=1, tiled=True).astype(jnp.float32),
        precision=full_precision,
    )
    operator = lax.psum(partial_op, "silo")
    right_side = summed_on_arrival(partial_rhs, "silo", 1)

    def apply_cols(direction):
        return jnp.dot(operator, gathered_copies(direction, ROW, 0), precision=full_precision)

    def squares_cols(values):
        return one_axis_at_a_time(values, ROW)

    def curv_values(values):
        return one_axis_at_a_time(values, ROW)

    solution = conj_grad(right_side, apply_cols, squares_cols, curv_values)
    transposed = solution.T
    return lax.all_to_all(transposed, ROW, split_axis=0, concat_axis=1, tiled=True)


def solution(mesh):
    torus = Mesh(mesh.devices.reshape(mesh.shape["silo"], 4, 4), ("silo", "row_0", "row_1"))
    in_specs = (P("silo", ROW, None), P("silo", ROW, None))
    out_specs = P(SILO_ROW, None)
    return jax.shard_map(local, mesh=torus, in_specs=in_specs, out_specs=out_specs, check_vma=False)
```

profile of v0, /device:TPU:0, one launch (start us, length us, event | category | flops | bytes accessed | tf_op | source)
XLA Modules:
  0.0 250.4 jit_solution(15347304648735894825)
XLA Ops:
  7.4 0.7 all-gather.2.cloned.1.call-update
  8.1 6.4 %reduce_sum.56 = f32[256,4096]{1,0:T(8,128)} reduce(f32[2,256,4096]{2,1,0:T(8,128)} %param.2, f32[]{:T(128)} %constant.0.clone.1), dimensions={0}, to_apply=%region_4.0 | reduce | flops 1048576 | bytes 12582916 | tf_op jit(solution)/shard_map/reduce_sum | solution.py:64
  14.6 78.5 %all-gather.2.cloned.1.call-done = bf16[2,4096,640]{2,1,0:T(8,128)(2,1)} async-done(((bf16[2,256,640]{2,1,0:T(8,128)(2,1)}), bf16[2,4096,640]{2,1,0:T(8,128)(2,1)}) %all-gather.2.cloned.1.call-update) | async-done | bytes 10485776 | tf_op jit(solution)/shard_map/all_gather | solution.py:68
  93.1 15.7 %fusion.1 = f32[256,640,1]{0,1,2:T(8,128)S(1)} fusion(f32[2,256,4096]{2,1,0:T(8,128)} %param.2, bf16[2,4096,640]{2,1,0:T(8,128)(2,1)} %all-gather.2.cloned.1.call-done), kind=kOutput, calls=%fused_computation.8 | convolution fusion | flops 16106127360 | bytes 19529728 | tf_op jit(solution)/shard_map/srk,skc->rc/dot_general | solution.py:65
  108.8 16.0 %all_to_all.34 = f32[8,256,80]{1,2,0:T(8,128)S(1)} all-to-all(f32[8,256,80]{1,2,0:T(8,128)S(1)} %bitcast.24), channel_id=1, replica_groups=mesh['silo'=8,'row_0'=4,'row_1'=4] {'silo'}, dimensions={0} | all-to-all | bytes 1310720 | tf_op jit(solution)/shard_map/all_to_all | solution.py:21
  124.9 0.1 broadcast_in_dim.4
  125.0 24.9 %all_to_all.35 = f32[16,256,80]{1,2,0:T(8,128)S(1)} all-to-all(f32[16,256,80]{1,2,0:T(8,128)S(1)} %broadcast_in_dim.4), channel_id=1, replica_groups=mesh['silo'=8,'row_0'=4,'row_1'=4] {'row_0','row_1'}, dimensions={0} | all-to-all | bytes 2621440 | tf_op jit(solution)/shard_map/all_to_all | solution.py:33
  149.9 0.1 copy.14
  150.0 6.2 %multiply_reduce_fusion.1 = (f32[80]{0:T(128)S(1)}, f32[80]{0:T(128)S(1)}, f32[256,80]{0,1:T(8,128)S(1)}) fusion(f32[256,80]{0,1:T(8,128)S(1)} %reduce_sum.54, f32[256,4096]{1,0:T(8,128)} %all-reduce.4.cloned.1.call-done, f32[4096,80]{0,1:T(8,128)S(1)} %bitcast.22), kind=kOutput, calls=%fused_computation.6 | convolution fusion | flops 1006714752 | bytes 5669504 | tf_op jit(solution)/shard_map/dot_general | solution.py:75
  156.3 8.6 %all-reduce.1 = (f32[80]{0:T(128)S(1)}, f32[80]{0:T(128)S(1)}) all-reduce(f32[80]{0:T(128)S(1)} %get-tuple-element.6, f32[80]{0:T(128)S(1)} %get-tuple-element.5), channel_id=1, replica_groups=mesh['silo'=8,'row_0'=4,'row_1'=4] {'row_0'}, use_global_device_ids=true, to_apply=%region_2.0 | all-reduce | flops 160 | bytes 1280 | tf_op jit(solution)/shard_map/psum | solution.py:42
  164.9 8.7 %all-reduce = (f32[80]{0:T(128)S(1)}, f32[80]{0:T(128)S(1)}) all-reduce(f32[80]{0:T(128)S(1)} %get-tuple-element.9, f32[80]{0:T(128)S(1)} %get-tuple-element.10), channel_id=1, replica_groups=mesh['silo'=8,'row_0'=4,'row_1'=4] {'row_1'}, use_global_device_ids=true, to_apply=%region_3.0 | all-reduce | flops 160 | bytes 1280 | tf_op jit(solution)/shard_map/psum | solution.py:42
  173.6 0.2 multiply_reduce_fusion
  173.8 8.6 %psum.68 = f32[80]{0:T(128)S(1)} all-reduce(f32[80]{0:T(128)S(1)} %multiply_reduce_fusion), channel_id=1, replica_groups=mesh['silo'=8,'row_0'=4,'row_1'=4] {'row_0'}, use_global_device_ids=true, to_apply=%region_10.0 | all-reduce | flops 80 | bytes 640 | tf_op jit(solution)/shard_map/psum | solution.py:42
  182.4 9.1 %psum.69 = f32[80]{0:T(128)S(1)} all-reduce(f32[80]{0:T(128)S(1)} %psum.68), channel_id=1, replica_groups=mesh['silo'=8,'row_0'=4,'row_1'=4] {'row_1'}, use_global_device_ids=true, to_apply=%region_11.0 | all-reduce | flops 80 | bytes 640 | tf_op jit(solution)/shard_map/psum | solution.py:42
  191.5 0.1 multiply_add_fusion
  191.6 0.1 broadcast_in_dim.5
  191.8 18.1 %all_to_all.36 = f32[16,256,80]{1,2,0:T(8,128)S(1)} all-to-all(f32[16,256,80]{1,2,0:T(8,128)S(1)} %broadcast_in_dim.5), channel_id=1, replica_groups=mesh['silo'=8,'row_0'=4,'row_1'=4] {'row_0','row_1'}, dimensions={0} | all-to-all | bytes 2621440 | tf_op jit(solution)/shard_map/all_to_all | solution.py:33
  209.9 0.1 copy.15
  210.0 4.0 %fusion = f32[80]{0:T(128)S(1)} fusion(f32[256,80]{0,1:T(8,128)S(1)} %multiply_add_fusion, f32[256,4096]{1,0:T(8,128)S(1)} %copy-done, f32[4096,80]{0,1:T(8,128)S(1)} %bitcast.23), kind=kOutput, calls=%fused_computation.1 | convolution fusion | flops 1006673856 | bytes 5587264 | tf_op jit(solution)/shard_map/dot_general | solution.py:75
  214.0 8.6 %psum.70 = f32[80]{0:T(128)S(1)} all-reduce(f32[80]{0:T(128)S(1)} %fusion), channel_id=1, replica_groups=mesh['silo'=8,'row_0'=4,'row_1'=4] {'row_0'}, use_global_device_ids=true, to_apply=%region_13.0 | all-reduce | flops 80 | bytes 640 | tf_op jit(solution)/shard_map/psum | solution.py:42
  222.6 8.7 %psum.71 = f32[80]{0:T(128)S(1)} all-reduce(f32[80]{0:T(128)S(1)} %psum.70), channel_id=1, replica_groups=mesh['silo'=8,'row_0'=4,'row_1'=4] {'row_1'}, use_global_device_ids=true, to_apply=%region_14.0 | all-reduce | flops 80 | bytes 640 | tf_op jit(solution)/shard_map/psum | solution.py:42
  231.3 0.1 add_bitcast_fusion
  231.5 10.8 %all_to_all.37 = f32[16,5,256]{2,1,0:T(8,128)S(1)} all-to-all(f32[16,5,256]{2,1,0:T(8,128)S(1)} %all_to_all.26), channel_id=1, replica_groups=mesh['silo'=8,'row_0'=4,'row_1'=4] {'row_0','row_1'}, dimensions={0} | all-to-all | bytes 163840 | tf_op jit(solution)/shard_map/all_to_all | solution.py:85
  242.3 0.7 copy.18
  (11 shorter events, 0.2 us)
Async XLA Ops:
  7.4 85.7 %all-gather.2.cloned.1.call-start = ((), (), s32[]{:S(2)}) async-start(), calls=%async_computation.4 | async-start | bytes 11141120 | tf_op jit(solution)/shard_map/all_gather | solution.py:68
  8.1 141.9 %all-reduce.4.cloned.1.call-start = ((), (), s32[]{:S(2)}) async-start(), calls=%async_computation.5 | async-start | bytes 8388608 | tf_op jit(solution)/shard_map/psum | solution.py:71
  191.5 18.5 %copy-start = (f32[256,4096]{1,0:T(8,128)S(1)}, f32[256,4096]{1,0:T(8,128)}, u32[]{:S(2)}) copy-start(f32[256,4096]{1,0:T(8,128)} %all-reduce.4.cloned.1.call-done) | copy-start | bytes 12582916
Sparse Core Ops, SparseCore 0:
  10.3 82.7 all-gather.1
Sparse Core Ops, SparseCore 1:
  14.7 76.3 all-reduce.3
where the time goes:
time: 251 us; the launch traced here: 250 us
  blocking collectives  122 us (49%)
  waiting for transfers between devices  79.3 us (32%)
  matrix products  26 us (10%)
  between operations  14.9 us (6%)
  other arithmetic  6.85 us (3%)
    all_gather x1, waiting for transfers between devices, local(): lax.all_gather(silo_weights, ROW, axis=1, tiled=True).astype(jnp.float32)  78.5 us
    psum x6, blocking collectives, one_axis_at_a_time(): value = lax.psum(value, axis)  52.3 us
    all_to_all x2, blocking collectives, sent_to_all(): return lax.all_to_all(copies, axis, split_axis=0, concat_axis=0, tiled=True)  43 us
    all_to_all x1, blocking collectives, summed_on_arrival(): lax.all_to_all(parts, axis, split_axis=0, concat_axis=0, tiled=True)  16 us
    dot_general x1, matrix products, local(): jnp.einsum('srk,skc->rc', silo_grams, lax.all_gather(silo_weights, ROW, a...  15.7 us
    all_to_all x1, blocking collectives, local(): lax.all_to_all(transposed, ROW, split_axis=0, concat_axis=1, tiled=True)  10.8 us
    dot_general x2, matrix products, apply_cols(): jnp.dot(operator, gathered_copies(direction, ROW, 0), precision=full_prec...  10.3 us
    reduce_sum x1, other arithmetic, local(): partial_op = jnp.sum(silo_grams, axis=0)  6.42 us
  transfers between devices with their start and end apart: 2, of which 1 were waited for; matrix products, arithmetic and copies ran while one was open for 9% of the time, Pallas kernels for 0%

commit v1 on v0

--- a/solution.py
+++ b/solution.py
@@ -61,11 +61,24 @@
 
 
 def local(silo_grams, silo_weights):
+
+    def _match_stacks_all(vec, axis_name):
+        spare = jnp.concatenate(
+            lax.all_to_all(
+                jnp.stack(tuple((vec for _ in range(lax.psum(1, axis_name))))),
+                axis_name=axis_name,
+                split_axis=0,
+                concat_axis=0,
+            ),
+            axis=1,
+        )
+        return spare
+
     partial_op = jnp.sum(silo_grams, axis=0)
     partial_rhs = jnp.einsum(
         "srk,skc->rc",
         silo_grams,
-        lax.all_gather(silo_weights, ROW, axis=1, tiled=True).astype(jnp.float32),
+        _match_stacks_all(silo_weights, ROW).astype(jnp.float32),
         precision=full_precision,
     )
     operator = lax.psum(partial_op, "silo")

time: 251 us -> 355 us (1.41)
  waiting for transfers between devices: 79.3 us -> 149 us
  local copies, waits for them, and re-layouts: 1.16 us -> 31.6 us
  starting transfers between devices: 0.05 us -> 7.2 us
    all_to_all x0 -> x1, waiting for transfers between devices: none -> 149 us  [_match_stacks_all(): lax.all_to_all(jnp.stack(tuple((vec for _ in range(lax.psum(1, axis_name)...]
    all_gather x1 -> x0, waiting for transfers between devices: 78.5 us -> none  [local(): lax.all_gather(silo_weights, ROW, axis=1, tiled=True).astype(jnp.float32)]
    dot_general x0 -> x1, local copies, waits for them, and re-layouts: none -> 14.7 us  [local(): jnp.einsum('srk,skc->rc', silo_grams, _match_stacks_all(silo_weights, ROW...]
    all_to_all x0 -> x1, local copies, waits for them, and re-layouts: none -> 9.4 us  [_match_stacks_all(): lax.all_to_all(jnp.stack(tuple((vec for _ in range(lax.psum(1, axis_name)...]
    all_to_all x0 -> x1, starting transfers between devices: none -> 7.16 us  [_match_stacks_all(): lax.all_to_all(jnp.stack(tuple((vec for _ in range(lax.psum(1, axis_name)...]
    another operation x0 -> x1, local copies, waits for them, and re-layouts: none -> 6.34 us  [_match_stacks_all(): jnp.stack(tuple((vec for _ in range(lax.psum(1, axis_name)))))]
  transfers between devices with their start and end apart: 2 -> 2, of which waited for: 1 -> 1; matrix products, arithmetic and copies ran while one was open for 9% -> 12% of each run, Pallas kernels for 0% -> 0%
where the time goes in v1:
time: 355 us; the launch traced here: 354 us
  waiting for transfers between devices  149 us (42%)
  blocking collectives  123 us (35%)
  local copies, waits for them, and re-layouts  31.6 us (9%)
  matrix products  22.7 us (6%)
  between operations  13.5 us (4%)
  starting transfers between devices  7.2 us (2%)
  other arithmetic  6.85 us (2%)
    all_to_all x1, waiting for transfers between devices, _match_stacks_all(): lax.all_to_all(jnp.stack(tuple((vec for _ in range(lax.psum(1, axis_name)...  149 us
    psum x6, blocking collectives, one_axis_at_a_time(): value = lax.psum(value, axis)  52.4 us
    all_to_all x2, blocking collectives, sent_to_all(): return lax.all_to_all(copies, axis, split_axis=0, concat_axis=0, tiled=True)  42.9 us
    all_to_all x1, blocking collectives, summed_on_arrival(): lax.all_to_all(parts, axis, split_axis=0, concat_axis=0, tiled=True)  16.9 us
    dot_general x1, local copies, waits for them, and re-layouts, local(): jnp.einsum('srk,skc->rc', silo_grams, _match_stacks_all(silo_weights, ROW...  14.7 us
    dot_general x1, matrix products, local(): jnp.einsum('srk,skc->rc', silo_grams, _match_stacks_all(silo_weights, ROW...  12.4 us
    all_to_all x1, blocking collectives, local(): lax.all_to_all(transposed, ROW, split_axis=0, concat_axis=1, tiled=True)  10.8 us
    dot_general x2, matrix products, apply_cols(): jnp.dot(operator, gathered_copies(direction, ROW, 0), precision=full_prec...  10.3 us
  transfers between devices with their start and end apart: 2, of which 1 were waited for; matrix products, arithmetic and copies ran while one was open for 12% of the time, Pallas kernels for 0%

profile of v1, /device:TPU:0, one launch (start us, length us, event | category | flops | bytes accessed | tf_op | source)
XLA Modules:
  0.0 353.7 jit_solution(7727881292983721413)
XLA Ops:
  6.5 6.3 %stack.2 = bf16[16,2,256,640]{3,2,1,0:T(8,128)(2,1)} broadcast(bf16[2,256,640]{2,1,0:T(8,128)(2,1)} %param.3), dimensions={1,2,3} | broadcast | bytes 11141120 | tf_op jit(solution)/shard_map/stack | solution.py:68
  12.9 7.2 %all-to-all-start = ((bf16[16,2,256,640]{3,2,1,0:T(8,128)(2,1)}), bf16[16,2,256,640]{3,2,1,0:T(8,128)(2,1)}, u32[]{:S(2)}, u32[]{:S(2)}) async-start(bf16[16,2,256,640]{3,2,1,0:T(8,128)(2,1)} %stack.2), calls=%async_computation | async-start | bytes 20971520 | tf_op jit(solution)/shard_map/all_to_all | solution.py:67
  20.1 6.4 %reduce_sum.56 = f32[256,4096]{1,0:T(8,128)} reduce(f32[2,256,4096]{2,1,0:T(8,128)} %param.2, f32[]{:T(128)} %constant.0.clone.1), dimensions={0}, to_apply=%region_4.0 | reduce | flops 1048576 | bytes 12582916 | tf_op jit(solution)/shard_map/reduce_sum | solution.py:77
  26.5 148.9 %all-to-all-done = bf16[16,2,256,640]{3,2,1,0:T(8,128)(2,1)} async-done(((bf16[16,2,256,640]{3,2,1,0:T(8,128)(2,1)}), bf16[16,2,256,640]{3,2,1,0:T(8,128)(2,1)}, u32[]{:S(2)}, u32[]{:S(2)}) %all-to-all-start) | async-done | bytes 10485792 | tf_op jit(solution)/shard_map/all_to_all | solution.py:67
  175.5 9.4 %copy.12 = bf16[16,2,256,640]{3,2,0,1:T(8,128)(2,1)} copy(bf16[16,2,256,640]{3,2,1,0:T(8,128)(2,1)} %all-to-all-done) | data formatting | bytes 20971520 | tf_op jit(solution)/shard_map/all_to_all | solution.py:67
  184.8 14.7 %copy.13 = bf16[640,4096,2]{1,0,2:T(8,128)(2,1)} copy(bf16[640,4096,2]{0,1,2:T(8,128)(2,1)} %bitcast.35) | data formatting | bytes 20971520 | tf_op jit(solution)/shard_map/srk,skc->rc/dot_general | solution.py:78
  199.6 12.4 %fusion.2 = f32[8,256,80]{1,2,0:T(8,128)S(1)} fusion(bf16[8,80,4096,2]{2,1,0,3:T(8,128)(2,1)} %bitcast.36, f32[2,256,4096]{2,1,0:T(8,128)} %param.2), kind=kOutput, calls=%fused_computation.2 | convolution fusion | flops 16106127360 | bytes 19529728 | tf_op jit(solution)/shard_map/srk,skc->rc/dot_general | solution.py:78
  212.0 16.9 %all_to_all.39 = f32[8,256,80]{1,2,0:T(8,128)S(1)} all-to-all(f32[8,256,80]{1,2,0:T(8,128)S(1)} %fusion.2), channel_id=1, replica_groups=mesh['silo'=8,'row_0'=4,'row_1'=4] {'silo'}, dimensions={0} | all-to-all | bytes 1310720 | tf_op jit(solution)/shard_map/all_to_all | solution.py:21
  229.0 0.1 broadcast_in_dim.4
  229.1 24.8 %all_to_all.40 = f32[16,256,80]{1,2,0:T(8,128)S(1)} all-to-all(f32[16,256,80]{1,2,0:T(8,128)S(1)} %broadcast_in_dim.4), channel_id=1, replica_groups=mesh['silo'=8,'row_0'=4,'row_1'=4] {'row_0','row_1'}, dimensions={0} | all-to-all | bytes 2621440 | tf_op jit(solution)/shard_map/all_to_all | solution.py:33
  253.9 0.1 copy.18
  254.0 6.2 %multiply_reduce_fusion.1 = (f32[80]{0:T(128)S(1)}, f32[80]{0:T(128)S(1)}, f32[256,80]{0,1:T(8,128)S(1)}) fusion(f32[256,80]{0,1:T(8,128)S(1)} %reduce_sum.54, f32[256,4096]{1,0:T(8,128)} %all-reduce.4.cloned.1.call-done, f32[4096,80]{0,1:T(8,128)S(1)} %bitcast.39), kind=kOutput, calls=%fused_computation.9 | convolution fusion | flops 1006714752 | bytes 5669504 | tf_op jit(solution)/shard_map/dot_general | solution.py:88
  260.3 8.6 %all-reduce.1 = (f32[80]{0:T(128)S(1)}, f32[80]{0:T(128)S(1)}) all-reduce(f32[80]{0:T(128)S(1)} %get-tuple-element.6, f32[80]{0:T(128)S(1)} %get-tuple-element.5), channel_id=1, replica_groups=mesh['silo'=8,'row_0'=4,'row_1'=4] {'row_0'}, use_global_device_ids=true, to_apply=%region_2.0 | all-reduce | flops 160 | bytes 1280 | tf_op jit(solution)/shard_map/psum | solution.py:42
  268.9 8.7 %all-reduce = (f32[80]{0:T(128)S(1)}, f32[80]{0:T(128)S(1)}) all-reduce(f32[80]{0:T(128)S(1)} %get-tuple-element.9, f32[80]{0:T(128)S(1)} %get-tuple-element.10), channel_id=1, replica_groups=mesh['silo'=8,'row_0'=4,'row_1'=4] {'row_1'}, use_global_device_ids=true, to_apply=%region_3.0 | all-reduce | flops 160 | bytes 1280 | tf_op jit(solution)/shard_map/psum | solution.py:42
  277.6 0.2 multiply_reduce_fusion
  277.8 8.6 %psum.68 = f32[80]{0:T(128)S(1)} all-reduce(f32[80]{0:T(128)S(1)} %multiply_reduce_fusion), channel_id=1, replica_groups=mesh['silo'=8,'row_0'=4,'row_1'=4] {'row_0'}, use_global_device_ids=true, to_apply=%region_10.0 | all-reduce | flops 80 | bytes 640 | tf_op jit(solution)/shard_map/psum | solution.py:42
  286.4 9.1 %psum.69 = f32[80]{0:T(128)S(1)} all-reduce(f32[80]{0:T(128)S(1)} %psum.68), channel_id=1, replica_groups=mesh['silo'=8,'row_0'=4,'row_1'=4] {'row_1'}, use_global_device_ids=true, to_apply=%region_11.0 | all-reduce | flops 80 | bytes 640 | tf_op jit(solution)/shard_map/psum | solution.py:42
  295.8 18.1 %all_to_all.41 = f32[16,256,80]{1,2,0:T(8,128)S(1)} all-to-all(f32[16,256,80]{1,2,0:T(8,128)S(1)} %broadcast_in_dim.5), channel_id=1, replica_groups=mesh['silo'=8,'row_0'=4,'row_1'=4] {'row_0','row_1'}, dimensions={0} | all-to-all | bytes 2621440 | tf_op jit(solution)/shard_map/all_to_all | solution.py:33
  313.8 0.1 copy.19
  314.0 4.0 %fusion.5 = f32[80]{0:T(128)S(1)} fusion(f32[256,80]{0,1:T(8,128)S(1)} %multiply_add_fusion, f32[256,4096]{1,0:T(8,128)S(1)} %copy-done, f32[4096,80]{0,1:T(8,128)S(1)} %bitcast.40), kind=kOutput, calls=%fused_computation.4 | convolution fusion | flops 1006673856 | bytes 5587264 | tf_op jit(solution)/shard_map/dot_general | solution.py:88
  318.0 8.6 %psum.70 = f32[80]{0:T(128)S(1)} all-reduce(f32[80]{0:T(128)S(1)} %fusion.5), channel_id=1, replica_groups=mesh['silo'=8,'row_0'=4,'row_1'=4] {'row_0'}, use_global_device_ids=true, to_apply=%region_13.0 | all-reduce | flops 80 | bytes 640 | tf_op jit(solution)/shard_map/psum | solution.py:42
  326.6 8.7 %psum.71 = f32[80]{0:T(128)S(1)} all-reduce(f32[80]{0:T(128)S(1)} %psum.70), channel_id=1, replica_groups=mesh['silo'=8,'row_0'=4,'row_1'=4] {'row_1'}, use_global_device_ids=true, to_apply=%region_14.0 | all-reduce | flops 80 | bytes 640 | tf_op jit(solution)/shard_map/psum | solution.py:42
  335.4 10.8 %all_to_all.42 = f32[16,5,256]{2,1,0:T(8,128)S(1)} all-to-all(f32[16,5,256]{2,1,0:T(8,128)S(1)} %all_to_all.30), channel_id=1, replica_groups=mesh['silo'=8,'row_0'=4,'row_1'=4] {'row_0','row_1'}, dimensions={0} | all-to-all | bytes 163840 | tf_op jit(solution)/shard_map/all_to_all | solution.py:98
  346.2 0.7 copy.22
  (13 shorter events, 0.5 us)
Async XLA Ops:
  12.9 162.6 %all-to-all-start = ((bf16[16,2,256,640]{3,2,1,0:T(8,128)(2,1)}), bf16[16,2,256,640]{3,2,1,0:T(8,128)(2,1)}, u32[]{:S(2)}, u32[]{:S(2)}) async-start(bf16[16,2,256,640]{3,2,1,0:T(8,128)(2,1)} %stack.2), calls=%async_computation | async-start | bytes 20971520 | tf_op jit(solution)/shard_map/all_to_all | solution.py:67
  20.0 234.0 %all-reduce.4.cloned.1.call-start = ((), (), s32[]{:S(2)}) async-start(), calls=%async_computation.5 | async-start | bytes 8388608 | tf_op jit(solution)/shard_map/psum | solution.py:84
  295.5 18.5 %copy-start = (f32[256,4096]{1,0:T(8,128)S(1)}, f32[256,4096]{1,0:T(8,128)}, u32[]{:S(2)}) copy-start(f32[256,4096]{1,0:T(8,128)} %all-reduce.4.cloned.1.call-done) | copy-start | bytes 12582916
Sparse Core Ops, SparseCore 0:
  26.7 77.1 all-reduce.3
